TPU v7x, 256 devices: a whole 4x4x8 slice. The times are simulated.
256 devices in a mesh: dp: 8 (over y, core), mp: 32 (over z, x).
Axes of the slice: x: 4, y: 4, z: 8, core: 2. Of those that a mesh axis runs over, the one named last changes fastest.
Arguments:
- tokens: bfloat16 [4096, 12288], P(('dp', 'mp')), may hold values from -6 to 6
- block_weights: float32 [384, 8, 128, 128], P('mp'), may hold values from -0.1875 to 0.1875
- block_rows: int32 [384, 8], P('mp'), may hold values from 0 to 95, all different within a row
- block_owners: int32 [384, 8, 1], P('mp'), may hold values from 0 to 7; in each aligned block of 96 rows (0 to 95, 96 to 191, ..., all dimensions but the last counted through in order) at most 18 rows name the same one
- factor_in: float32 [12288, 128], P('mp'), may hold values from -0.0546875 to 0.0546875
- factor_out: float32 [128, 49152], P(None, 'mp'), may hold values from -0.5 to 0.5
- upstream: bfloat16 [4096, 49152], P('dp', 'mp'), may hold values from -0.09375 to 0.09375
Outputs:
- hidden: bfloat16 [4096, 49152], P('dp', 'mp')
- block_grads: float32 [4608, 128, 128], P(('mp', 'dp'))
- factor_in_grad: float32 [12288, 128], P(('mp', 'dp'))
- factor_out_grad: float32 [128, 49152], P(None, ('mp', 'dp'))
Inputs may be any that keep to these rules, and one draw needn't show every extreme that they name: `block_rows`: each column block names 8 different row blocks. `block_owners`: among the 96 active blocks of one index of mp (aligned runs of 12 column blocks), one index of dp owns at most 18; in some runs one owns exactly 18.
All inputs are finite; a program needn't handle non-finite values.
Results may differ from a plain program's by a relative error of at most 0.001.
Values may be sent and summed in bfloat16 or wider, within the bound.
No kernel may reach another device: no remote copies, remote signals or barrier semaphores. Data moves between devices by JAX's collectives and lax.ppermute only.
A program may use at most 128 MiB of HBM per device.

v0:
```python
import jax
import jax.numpy as jnp
from jax import lax
from jax.sharding import PartitionSpec as P

highest = lax.Precision.HIGHEST


def gelu_tanh(values):
    return jax.nn.gelu(values, approximate=True)


def per_device(tokens, block_weights, block_rows, block_owners, factor_in, factor_out, upstream):
    block_size = block_weights.shape[-1]
    col_blocks = block_rows.shape[0]
    per_col = block_rows.shape[1]
    gathered = lax.all_gather(tokens, "mp", axis=0, tiled=True)
    row_total = gathered.shape[0]
    width = gathered.shape[1]
    slice_width = factor_in.shape[0]
    col_start = lax.axis_index("mp") * slice_width
    own_cols = lax.dynamic_slice_in_dim(gathered, col_start, slice_width, 1).astype(jnp.float32)
    low_act = lax.psum(jnp.dot(own_cols, factor_in, precision=highest), "mp")
    feature_blocks = gathered.reshape(row_total, width // block_size, block_size)
    panels = jnp.take(feature_blocks, block_rows.reshape(-1), axis=1).astype(jnp.float32)
    panels = panels.reshape(row_total, col_blocks, per_col, block_size)
    sparse = jnp.einsum("tckb,ckbo->tco", panels, block_weights, precision=highest)
    preact = sparse.reshape(row_total, col_blocks * block_size) + jnp.dot(
        low_act, factor_out, precision=highest
    )
    hidden, pullback = jax.vjp(gelu_tanh, preact)
    pre_grad = pullback(upstream.astype(jnp.float32))[0]
    weight_grad = jnp.einsum(
        "tckb,tco->ckbo",
        panels,
        pre_grad.reshape(row_total, col_blocks, block_size),
        precision=highest,
    )
    back_low = lax.psum(jnp.dot(pre_grad, factor_out.T, precision=highest), "mp")
    in_part = jnp.dot(own_cols.T, back_low, precision=highest)
    out_part = jnp.dot(low_act.T, pre_grad, precision=highest)
    block_count = col_blocks * per_col
    block_grad = weight_grad.reshape(block_count, block_size, block_size)
    owners = block_owners.reshape(-1)
    groups = lax.axis_size("dp")
    capacity = max(2, 3 * block_count // (2 * groups))
    group_ids = jnp.arange(groups, dtype=jnp.int32)
    owner_marks = (owners[:, None] == group_ids[None, :]).astype(jnp.int32)
    earlier = jnp.cumsum(owner_marks, axis=0, dtype=jnp.int32) - owner_marks
    slot_rank = jnp.sum(earlier * owner_marks, axis=1, dtype=jnp.int32)
    own_index = lax.axis_index("dp")
    chosen = (owners[None, :] == own_index) & (
        slot_rank[None, :] == jnp.arange(capacity, dtype=jnp.int32)[:, None]
    )
    where_idx = jnp.sum(
        chosen.astype(jnp.int32) * jnp.arange(block_count, dtype=jnp.int32)[None, :],
        axis=1,
        dtype=jnp.int32,
    )
    present = jnp.any(chosen, axis=1)
    reduced, in_grad, out_grad = (
        lax.psum_scatter(block_grad, "dp", scatter_dimension=0, tiled=True),
        lax.psum_scatter(in_part, "dp", scatter_dimension=0, tiled=True),
        lax.psum_scatter(out_part, "dp", scatter_dimension=1, tiled=True),
    )
    summed = lax.all_gather(reduced, "dp", axis=0, tiled=True)
    grad_slots = jnp.where(present[:, None, None], summed[where_idx], 0.0)
    return (hidden.astype(jnp.bfloat16), grad_slots, in_grad, out_grad)


def solution(mesh):
    return jax.shard_map(
        per_device,
        mesh=mesh,
        in_specs=(
            P(("dp", "mp"), None),
            P("mp", None, None, None),
            P("mp", None),
            P("mp", None, None),
            P("mp", None),
            P(None, "mp"),
            P("dp", "mp"),
        ),
        out_specs=(
            P("dp", "mp"),
            P(("mp", "dp"), None, None),
            P(("mp", "dp"), None),
            P(None, ("mp", "dp")),
        ),
        check_vma=False,
    )
```

profile of v0, /device:TPU:1, one launch (start us, length us, event | category | flops | bytes accessed | tf_op | source)
XLA Modules:
  0.0 615.0 jit_solution(555664460729309711)
XLA Ops:
  7.2 0.7 all-gather.3.cloned.1.call-update
  8.0 0.8 copy.52
  8.7 0.7 compare_and_fusion
  9.4 0.1 copy.50
  9.6 124.1 %all-gather.3.cloned.1.call-done = bf16[512,12288]{1,0:T(8,128)(2,1)} async-done(((bf16[16,12288]{1,0:T(8,128)(2,1)}), bf16[512,12288]{1,0:T(8,128)(2,1)}) %all-gather.3.cloned.1.call-update) | async-done | bytes 12582928 | tf_op jit(solution)/shard_map/all_gather | solution.py:17
  133.7 2.2 fusion.15
  136.0 16.7 %copy.51 = bf16[512,12288]{0,1:T(8,128)(2,1)} copy(bf16[512,12288]{1,0:T(8,128)(2,1)} %all-gather.3.cloned.1.call-done) | data formatting | bytes 25165824 | tf_op jit(solution)/shard_map/all_gather | solution.py:17
  152.6 16.6 %copy.53 = bf16[512,96,128]{2,0,1:T(8,128)(2,1)} copy(bf16[512,96,128]{0,2,1:T(8,128)(2,1)} %bitcast.34) | data formatting | bytes 25165824 | tf_op jit(solution)/shard_map/reshape | solution.py:24
  169.2 11.5 %gather_fusion = bf16[96,512,128]{2,1,0:T(8,128)(2,1)} fusion(bf16[512,96,128]{2,0,1:T(8,128)(2,1)} %copy.53, s32[1024]{0:T(1024)S(1)} %pad_clamp_fusion.1), kind=kCustom, calls=%fused_computation | custom fusion | bytes 25166208 | tf_op jit(solution)/shard_map/jit(_take)/gather | solution.py:25
  180.7 16.7 %copy.54 = bf16[512,12,8,128]{0,3,2,1:T(8,128)(2,1)} copy(bf16[512,12,8,128]{3,0,2,1:T(8,128)(2,1)} %bitcast.35) | data formatting | bytes 25165824 | tf_op jit(solution)/shard_map/jit(_take)/gather | solution.py:25
  197.4 16.3 %fusion.1 = f32[12,512,128,1]{1,2,3,0:T(8,128)} fusion(f32[12,8,128,128]{3,2,1,0:T(8,128)} %param.8, bf16[512,12,8,128]{0,3,2,1:T(8,128)(2,1)} %copy.54, pred[12,8]{1,0:T(8,128)(4,1)S(1)} %copy.50), kind=kOutput, calls=%fused_computation.4 | convolution fusion | flops 9669967872 | bytes 22020192 | tf_op jit(solution)/shard_map/tckb,ckbo->tco/dot_general | solution.py:27
  213.8 3.7 copy.57
  217.5 57.3 %all-reduce.3.cloned.1.call-done = f32[512,128]{1,0:T(8,128)} async-done(((f32[512,128]{1,0:T(8,128)}), f32[512,128]{1,0:T(8,128)}) %all-reduce.3.cloned.1.call-update) | async-done | bytes 262160 | tf_op jit(solution)/shard_map/psum | solution.py:23
  274.8 7.9 %fusion.5 = (f32[512,1536]{1,0:T(8,128)}, bf16[512,1536]{1,0:T(8,128)(2,1)}) fusion(bf16[512,1536]{1,0:T(8,128)(2,1)S(1)} %copy-done.3, f32[512,1536]{1,0:T(8,128)} %copy.57, f32[512,128]{1,0:T(8,128)} %all-reduce.3.cloned.1.call-done, f32[128,1536]{1,0:T(8,128)S(1)} %copy-done), kind=kOutput, calls=%fused_computation.13 | convolution fusion | flops 1226047488 | bytes 10485760 | tf_op jit(solution)/shard_map/dot_general | solution.py:28
  282.7 3.5 copy.59
  286.2 15.7 %fusion = f32[12,8,128,128]{3,2,1,0:T(8,128)} fusion(f32[512,12,128,1]{0,2,3,1:T(8,128)} %bitcast.37, bf16[512,12,8,128]{0,3,2,1:T(8,128)(2,1)} %copy.54, pred[12,8]{1,0:T(8,128)(4,1)S(1)} %copy.50), kind=kOutput, calls=%fused_computation.3 | convolution fusion | flops 9669967872 | bytes 22020192 | tf_op jit(solution)/shard_map/tckb,tco->ckbo/dot_general | solution.py:33
  302.0 5.2 fusion.26
  307.3 40.7 %reduce-scatter.4.cloned.1.call-done = f32[12,128,128]{2,1,0:T(8,128)} async-done(((f32[96,128,128]{2,1,0:T(8,128)}), f32[12,128,128]{2,1,0:T(8,128)}) %reduce-scatter.4.cloned.1.call-update) | async-done | bytes 786448 | tf_op jit(solution)/shard_map/reduce_scatter | solution.py:62
  348.1 143.7 %all-reduce.5.cloned.1.call-done = f32[512,128]{1,0:T(8,128)} async-done(((f32[512,128]{1,0:T(8,128)}), f32[512,128]{1,0:T(8,128)}) %all-reduce.5.cloned.1.call-update) | async-done | bytes 262160 | tf_op jit(solution)/shard_map/psum | solution.py:39
  491.7 2.3 fusion.13
  494.1 0.3 reduce-scatter.8.cloned.1.call-start
  494.4 7.8 %fusion.27 = f32[128,1536]{0,1:T(8,128)} fusion(f32[512,128]{1,0:T(8,128)S(1)} %copy-done.1, f32[512,1536]{1,0:T(8,128)} %get-tuple-element.4), kind=kOutput, calls=%fused_computation.48 | convolution fusion | flops 1207959552 | bytes 4194304 | tf_op jit(solution)/shard_map/dot_general | solution.py:41
  502.4 0.1 fusion.17
  502.5 0.1 reduce_window_sum.11
  502.7 0.2 select_reduce_fusion
  502.9 0.1 select_reduce_fusion.1
  503.0 0.1 fusion.19
  503.1 35.7 %all-gather.5.cloned.1.call-done = f32[96,128,128]{2,1,0:T(8,128)} async-done(((f32[12,128,128]{2,1,0:T(8,128)}), f32[96,128,128]{2,1,0:T(8,128)}) %all-gather.5.cloned.1.call-update) | async-done | bytes 6291472 | tf_op jit(solution)/shard_map/all_gather | solution.py:66
  538.8 3.4 gather_fusion.1
  542.2 1.2 broadcast_select_fusion.3
  543.4 28.7 %reduce-scatter.6.cloned.1.call-done = f32[48,128]{1,0:T(8,128)} async-done(((f32[384,128]{1,0:T(8,128)}), f32[48,128]{1,0:T(8,128)}) %reduce-scatter.6.cloned.1.call-update) | async-done | bytes 24592 | tf_op jit(solution)/shard_map/reduce_scatter | solution.py:63
  572.1 36.1 %reduce-scatter.8.cloned.1.call-done = f32[128,192]{0,1:T(8,128)} async-done(((f32[128,1536]{0,1:T(8,128)}), f32[128,192]{0,1:T(8,128)}) %reduce-scatter.8.cloned.1.call-update) | async-done | bytes 98320 | tf_op jit(solution)/shard_map/reduce_scatter | solution.py:64
  (28 shorter events, 0.6 us)
Async XLA Ops:
  7.2 267.6 %copy-start = (f32[128,1536]{1,0:T(8,128)S(1)}, f32[128,1536]{1,0:T(8,128)}, u32[]{:S(2)}) copy-start(f32[128,1536]{1,0:T(8,128)} %param.12) | copy-start | bytes 2359300
  7.2 126.5 %all-gather.3.cloned.1.call-start = ((), (), s32[]{:S(2)}) async-start(), calls=%async_computation.3 | async-start | bytes 12976128 | tf_op jit(solution)/shard_map/all_gather | solution.py:17
  7.9 266.9 %all-reduce.3.cloned.1.call-start = ((), (), s32[]{:S(2)}) async-start(), calls=%async_computation.4 | async-start | bytes 524288 | tf_op jit(solution)/shard_map/psum | solution.py:23
  135.9 212.1 %reduce-scatter.4.cloned.1.call-start = ((), (), s32[]{:S(2)}) async-start(), calls=%async_computation.5 | async-start | bytes 7077888 | tf_op jit(solution)/shard_map/reduce_scatter | solution.py:62
  213.7 61.0 %copy-start.3 = (bf16[512,1536]{1,0:T(8,128)(2,1)S(1)}, bf16[512,1536]{1,0:T(8,128)(2,1)}, u32[]{:S(2)}) copy-start(bf16[512,1536]{1,0:T(8,128)(2,1)} %param.13) | copy-start | bytes 4718596
  301.9 192.4 %copy-start.1 = (f32[512,128]{1,0:T(8,128)S(1)}, f32[512,128]{1,0:T(8,128)}, u32[]{:S(2)}) copy-start(f32[512,128]{1,0:T(8,128)} %all-reduce.3.cloned.1.call-done) | copy-start | bytes 786436
  301.9 189.8 %all-reduce.5.cloned.1.call-start = ((), (), s32[]{:S(2)}) async-start(), calls=%async_computation.7 | async-start | bytes 524288 | tf_op jit(solution)/shard_map/psum | solution.py:39
  307.3 231.5 %all-gather.5.cloned.1.call-start = ((), (), s32[]{:S(2)}) async-start(), calls=%async_computation.6 | async-start | bytes 7077888 | tf_op jit(solution)/shard_map/all_gather | solution.py:66
  348.0 154.2 %copy-start.2 = (s32[12,8,1]{0,2,1:T(1,128)S(1)}, s32[12,8,1]{0,2,1:T(1,128)}, u32[]{:S(2)}) copy-start(s32[12,8,1]{0,2,1:T(1,128)} %param.10) | copy-start | bytes 1156
  348.0 224.1 %reduce-scatter.6.cloned.1.call-start = ((), (), s32[]{:S(2)}) async-start(), calls=%async_computation.8 | async-start | bytes 221184 | tf_op jit(solution)/shard_map/reduce_scatter | solution.py:63
  494.1 114.1 %reduce-scatter.8.cloned.1.call-start = ((), (), s32[]{:S(2)}) async-start(), calls=%async_computation.9 | async-start | bytes 884736 | tf_op jit(solution)/shard_map/reduce_scatter | solution.py:64
Sparse Core Ops, SparseCore 0:
  10.6 123.0 all-gather.2
  137.7 137.0 all-reduce.2
  302.1 45.8 reduce-scatter.3
  351.9 139.8 all-reduce.4
  493.4 45.3 all-gather.4
  541.7 30.3 reduce-scatter.5
  575.4 32.7 reduce-scatter.7
where the time goes:
time: 618 us; the launch traced here: 615 us
  waiting for transfers between devices  467 us (76%)
  local copies, waits for them, and re-layouts  73.3 us (12%)
  matrix products  57.5 us (9%)
  between operations  14.2 us (2%)
    psum x1, waiting for transfers between devices, per_device(): lax.psum(jnp.dot(pre_grad, factor_out.T, precision=highest), 'mp')  144 us
    all_gather x1, waiting for transfers between devices, per_device(): gathered = lax.all_gather(tokens, 'mp', axis=0, tiled=True)  124 us
    psum x1, waiting for transfers between devices, per_device(): low_act = lax.psum(jnp.dot(own_cols, factor_in, precision=highest), 'mp')  57.3 us
    reduce_scatter x1, waiting for transfers between devices, per_device(): lax.psum_scatter(block_grad, 'dp', scatter_dimension=0, tiled=True)  40.7 us
    reduce_scatter x1, waiting for transfers between devices, per_device(): lax.psum_scatter(out_part, 'dp', scatter_dimension=1, tiled=True)  36.1 us
    all_gather x1, waiting for transfers between devices, per_device(): summed = lax.all_gather(reduced, 'dp', axis=0, tiled=True)  35.7 us
    reduce_scatter x1, waiting for transfers between devices, per_device(): lax.psum_scatter(in_part, 'dp', scatter_dimension=0, tiled=True)  28.7 us
    gather x2, local copies, waits for them, and re-layouts, per_device(): jnp.take(feature_blocks, block_rows.reshape(-1), axis=1).astype(jnp.float32)  28.2 us
  transfers between devices with their start and end apart: 7, of which 7 were waited for; matrix products, arithmetic and copies ran while one was open for 17% of the time, Pallas kernels for 0%

commit v1 on v0

v1 whole, which is shorter than its diff:
```python
import functools

import jax
import jax.numpy as jnp
from jax import lax
from jax.experimental import pallas as pl
from jax.experimental.pallas import tpu as pltpu
from jax.sharding import Mesh
from jax.sharding import PartitionSpec as P

highest = lax.Precision.HIGHEST
BS = 128
ROWS = 16
NX, NZ, NY, NC = 4, 8, 4, 2
COLS = 12
KB = 8
RB = 96
CAP = 18
GROUPS = NY * NC
SLOT_ROWS = CAP * BS
FO_ROWS = COLS * BS // GROUPS
CODE_ROWS = SLOT_ROWS + FO_ROWS
PART_ROWS = CODE_ROWS + 32
FINE = 256.0


def shift(axis, size, step):
    pairs = [(i, (i + step) % size) for i in range(size)]
    return lambda value: lax.ppermute(value, axis, pairs)


def split_two(value):
    high = value.astype(jnp.bfloat16)
    low = (value - high.astype(jnp.float32)).astype(jnp.bfloat16)
    return high, low


def level_of(block):
    top = jnp.max(jnp.abs(block), axis=0, keepdims=True)
    return jnp.ceil(jnp.log2(jnp.maximum(top, 1e-30)) * FINE)


def encode(block, level):
    inverse = jnp.exp2(level * (-1.0 / FINE)) * 32700.0
    return jnp.floor(block * inverse + 0.5).astype(jnp.int32).astype(jnp.int16)


def decode(code, level):
    unit = jnp.exp2(level * (1.0 / FINE)) * (1.0 / 32700.0)
    return code.astype(jnp.int32).astype(jnp.float32) * unit


def main_kernel(
    rows_ref, where_ref, place_ref, low_ref, weight_ref, factor_ref, up_ref, *rest
):
    pieces = rest[: NX * NZ]
    hidden_ref, send_ref, keep_ref, back_ref = rest[NX * NZ : NX * NZ + 4]
    tok, wide, low_two, codes, levels, sems = rest[NX * NZ + 4 :]
    c = pl.program_id(0)
    tokens = NX * NZ * ROWS

    @pl.when(c == 0)
    def _():
        for j in range(NX * NZ):
            pltpu.make_async_copy(pieces[j], tok.at[place_ref[j]], sems.at[j]).start()
        high, low = split_two(low_ref[...])
        low_two[:, :BS] = high
        low_two[:, BS:] = low
        wide[(KB + 1) * BS :, BS:] = jnp.zeros((BS, BS), jnp.bfloat16)
        back_ref[...] = jnp.zeros_like(back_ref)
        for j in range(NX * NZ):
            pltpu.make_async_copy(pieces[j], tok.at[place_ref[j]], sems.at[j]).wait()

    for k in range(KB):
        high, low = split_two(weight_ref[0, k])
        wide[k * BS : (k + 1) * BS, :BS] = high
        wide[k * BS : (k + 1) * BS, BS:] = low
    f_high, f_low = split_two(factor_ref[...])
    wide[KB * BS : (KB + 1) * BS, :BS] = f_high
    wide[KB * BS : (KB + 1) * BS, BS:] = f_low
    wide[(KB + 1) * BS :, :BS] = f_high

    panel = jnp.concatenate(
        [tok[:, rows_ref[c * KB + k]].reshape(tokens, BS) for k in range(KB)]
        + [low_two[...]],
        axis=1,
    )
    both = jnp.dot(panel, wide[...], preferred_element_type=jnp.float32)
    v = both[:, :BS] + both[:, BS:]
    root = 0.7978845608028654
    square = v * v
    t = jnp.tanh(root * v * (1.0 + 0.044715 * square))
    half = 0.5 * (1.0 + t)
    hidden_ref[...] = (v * half).astype(jnp.bfloat16)
    slope = half + 0.5 * root * v * (1.0 - t * t) * (1.0 + 3.0 * 0.044715 * square)
    grad = up_ref[...].astype(jnp.float32) * slope

    g_high, g_low = split_two(grad)
    g_two = jnp.concatenate([g_high, g_low], axis=1)
    f_two = jnp.concatenate(
        [
            jnp.concatenate([f_high, f_high], axis=1),
            jnp.concatenate([f_low, jnp.zeros_like(f_low)], axis=1),
        ],
        axis=0,
    )
    back = lax.dot_general(
        g_two, f_two, (((1,), (1,)), ((), ())), preferred_element_type=jnp.float32
    )
    back_ref[...] += back[:, :BS] + back[:, BS:]

    grad_t = grad.T
    t_high, t_low = split_two(grad_t)
    gt_two = jnp.concatenate([t_high, t_low], axis=0)
    product = jnp.dot(gt_two, panel, preferred_element_type=jnp.float32)
    product = product[:BS] + product[BS:]
    for k in range(KB):
        block = product[:, k * BS : (k + 1) * BS]
        level = level_of(block)
        part = where_ref[0, c * KB + k]
        slot = where_ref[1, c * KB + k]
        codes[part, pl.ds(pl.multiple_of(slot * BS, BS), BS)] = encode(block, level)
        levels[part, pl.ds(slot, 1)] = level
    outer = product[:, KB * BS : (KB + 1) * BS] + product[:, (KB + 1) * BS :]
    for h in range(2):
        block = outer[h * 64 : (h + 1) * 64]
        level = level_of(block)
        part = where_ref[2, c * 2 + h]
        slot = where_ref[3, c * 2 + h]
        start = pl.multiple_of(SLOT_ROWS + slot * 64, 64)
        codes[part, pl.ds(start, 64)] = encode(block, level)
        levels[part, pl.ds(CAP + slot, 1)] = level

    @pl.when(c == COLS - 1)
    def _():
        for part in range(2 * NY):
            codes[part, CODE_ROWS:] = levels[part].astype(jnp.int32).astype(jnp.int16)
        send = pltpu.make_async_copy(codes.at[pl.ds(0, NY)], send_ref, sems.at[0])
        keep = pltpu.make_async_copy(codes.at[pl.ds(NY, NY)], keep_ref, sems.at[1])
        send.start()
        keep.start()
        send.wait()
        keep.wait()


def blocks_of():
    spans = [(s * BS, BS, s) for s in range(CAP)]
    return spans + [(SLOT_ROWS + h * 64, 64, CAP + h) for h in range(FO_ROWS // 64)]


def pair_kernel(keep_ref, got_ref, out_ref):
    keep_levels = keep_ref[0, CODE_ROWS:].astype(jnp.int32).astype(jnp.float32)
    got_levels = got_ref[0, CODE_ROWS:].astype(jnp.int32).astype(jnp.float32)
    fresh = []
    for start, size, index in blocks_of():
        span = slice(start, start + size)
        total = decode(keep_ref[0, span], keep_levels[index : index + 1])
        total += decode(got_ref[0, span], got_levels[index : index + 1])
        level = level_of(total)
        out_ref[0, span] = encode(total, level)
        fresh.append(level)
    fresh.append(jnp.zeros((32 - len(fresh), BS), jnp.float32))
    fresh = jnp.concatenate(fresh, axis=0)
    out_ref[0, CODE_ROWS:] = fresh.astype(jnp.int32).astype(jnp.int16)


def final_kernel(count_ref, *refs):
    parts, (slots_ref, outer_ref) = refs[:NY], refs[NY:]
    levels = [p[CODE_ROWS:].astype(jnp.int32).astype(jnp.float32) for p in parts]
    count = count_ref[0]
    for start, size, index in blocks_of():
        span = slice(start, start + size)
        total = decode(parts[0][span], levels[0][index : index + 1])
        for i in range(1, NY):
            total += decode(parts[i][span], levels[i][index : index + 1])
        if index < CAP:
            slots_ref[index] = jnp.where(index < count, total.T, 0.0)
        else:
            h = index - CAP
            outer_ref[:, h * 64 : (h + 1) * 64] = total.T


def gather_tokens(own):
    z_up, z_down = shift("z", NZ, 1), shift("z", NZ, -1)
    x_up, x_down = shift("x", NX, 1), shift("x", NX, -1)
    across = shift("x", NX, 2)
    held = {(0, 0): own}
    held[0, 2] = across(own)
    for b in (0, 2):
        for a in (1, 2, 3):
            held[-a, b] = z_up(held[1 - a, b])
            held[a, b] = z_down(held[a - 1, b])
    held[4, 0] = z_up(held[-3, 0])
    held[4, 2] = z_down(held[3, 2])
    for a in (0, -1, 1, -2, 2, -3, 3, 4):
        for b, move in ((-1, x_up), (1, x_down)):
            if (a, b) in ((1, 1), (-1, -1)):
                held[a, b] = (z_down if a > 0 else z_up)(held[0, b])
            else:
                held[a, b] = move(held[a, 0])
    return held


def per_device(tokens, block_weights, block_rows, block_owners, factor_in, factor_out, upstream):
    own = jnp.transpose(tokens.reshape(ROWS, RB, BS), (1, 0, 2))
    held = gather_tokens(own)
    z, x = lax.axis_index("z"), lax.axis_index("x")
    y, core = lax.axis_index("y"), lax.axis_index("core")
    order = sorted(held)
    place = jnp.stack([((z + a) % NZ) * NX + (x + b) % NX for a, b in order]).astype(jnp.int32)
    pieces = [held[key] for key in order]

    plane = ("z", "x")
    span = NX * NZ
    per = RB // span
    own_cols = lax.all_to_all(own.reshape(span, per, ROWS, BS), plane, 0, 0)
    own_cols = own_cols.astype(jnp.float32)
    factor = factor_in.reshape(per, BS, BS)
    partial = jnp.einsum("sbtf,bfr->str", own_cols, factor, precision=highest)
    low_own = jnp.sum(lax.all_to_all(partial, plane, 0, 0), axis=0)
    low_act = lax.all_to_all(
        jnp.broadcast_to(low_own[None], (span, ROWS, BS)), plane, 0, 0
    ).reshape(span * ROWS, BS)

    owners = block_owners.reshape(-1)
    count_all = owners.shape[0]
    marks = (owners[:, None] == jnp.arange(GROUPS, dtype=jnp.int32)[None, :]).astype(jnp.int32)
    before = (
        jnp.arange(count_all, dtype=jnp.int32)[:, None]
        > jnp.arange(count_all, dtype=jnp.int32)[None, :]
    ) & (owners[:, None] == owners[None, :])
    rank = jnp.sum(before.astype(jnp.int32), axis=1)

    def part_of(owner):
        turn = (owner // NC - y) % NY
        return turn + jnp.where(owner % NC == core, NY, 0)

    halves = jnp.arange(2 * COLS, dtype=jnp.int32)
    per_owner = FO_ROWS // 64
    pad = count_all - 2 * COLS
    where = jnp.stack(
        [
            part_of(owners),
            rank,
            jnp.pad(part_of(halves // per_owner), (0, pad)),
            jnp.pad(halves % per_owner, (0, pad)),
        ]
    ).astype(jnp.int32)
    counts = jnp.sum(marks, axis=0)
    mine = jnp.sum(
        jnp.where(jnp.arange(GROUPS) == y * NC + core, counts, 0), dtype=jnp.int32
    ).reshape(1)

    total = span * ROWS
    anywhere = pl.BlockSpec(memory_space=pl.ANY)
    hidden, send, keep, back = pl.pallas_call(
        main_kernel,
        grid_spec=pltpu.PrefetchScalarGridSpec(
            num_scalar_prefetch=3,
            grid=(COLS,),
            in_specs=[
                pl.BlockSpec((total, BS), lambda c, *_: (0, 0)),
                pl.BlockSpec((1, KB, BS, BS), lambda c, *_: (c, 0, 0, 0)),
                pl.BlockSpec((BS, BS), lambda c, *_: (0, c)),
                pl.BlockSpec((total, BS), lambda c, *_: (0, c)),
            ]
            + [anywhere] * span,
            out_specs=[
                pl.BlockSpec((total, BS), lambda c, *_: (0, c)),
                anywhere,
                anywhere,
                pl.BlockSpec((total, BS), lambda c, *_: (0, 0)),
            ],
            scratch_shapes=[
                pltpu.VMEM((span, RB, ROWS, BS), jnp.bfloat16),
                pltpu.VMEM(((KB + 2) * BS, 2 * BS), jnp.bfloat16),
                pltpu.VMEM((total, 2 * BS), jnp.bfloat16),
                pltpu.VMEM((2 * NY, PART_ROWS, BS), jnp.int16),
                pltpu.VMEM((2 * NY, 32, BS), jnp.float32),
                pltpu.SemaphoreType.DMA((span,)),
            ],
        ),
        out_shape=[
            jax.ShapeDtypeStruct((total, COLS * BS), jnp.bfloat16),
            jax.ShapeDtypeStruct((NY, PART_ROWS, BS), jnp.int16),
            jax.ShapeDtypeStruct((NY, PART_ROWS, BS), jnp.int16),
            jax.ShapeDtypeStruct((total, BS), jnp.float32),
        ],
        compiler_params=pltpu.CompilerParams(vmem_limit_bytes=50 * 1024 * 1024),
        name="columns",
    )(
        block_rows.reshape(-1), where, place,
        low_act, block_weights, factor_out, upstream, *pieces,
    )

    got = shift("core", NC, 1)(send)
    paired = pl.pallas_call(
        pair_kernel,
        grid=(NY,),
        in_specs=[pl.BlockSpec((1, PART_ROWS, BS), lambda i: (i, 0, 0))] * 2,
        out_specs=pl.BlockSpec((1, PART_ROWS, BS), lambda i: (i, 0, 0)),
        out_shape=jax.ShapeDtypeStruct((NY, PART_ROWS, BS), jnp.int16),
        compiler_params=pltpu.CompilerParams(vmem_limit_bytes=50 * 1024 * 1024),
        name="pairs",
    )(keep, got)
    parts = [
        paired[0],
        shift("y", NY, 1)(paired[1]),
        shift("y", NY, 2)(paired[2]),
        shift("y", NY, 3)(paired[3]),
    ]

    back_own = jnp.sum(lax.all_to_all(back.reshape(span, ROWS, BS), plane, 0, 0), axis=0)
    back_all = lax.all_to_all(
        jnp.broadcast_to(back_own[None], (span, ROWS, BS)), plane, 0, 0
    )
    in_part = jnp.einsum("sbtf,str->bfr", own_cols, back_all, precision=highest)
    in_part = in_part.reshape(GROUPS, per * BS // GROUPS, BS)
    in_grad = jnp.sum(lax.all_to_all(in_part, ("y", "core"), 0, 0), axis=0)

    whole = pl.BlockSpec(memory_space=pltpu.VMEM)
    slots, out_grad = pl.pallas_call(
        final_kernel,
        in_specs=[pl.BlockSpec(memory_space=pltpu.SMEM)] + [whole] * NY,
        out_specs=[whole, whole],
        out_shape=[
            jax.ShapeDtypeStruct((CAP, BS, BS), jnp.float32),
            jax.ShapeDtypeStruct((BS, FO_ROWS), jnp.float32),
        ],
        compiler_params=pltpu.CompilerParams(vmem_limit_bytes=50 * 1024 * 1024),
        name="slots",
    )(mine, *parts)
    return hidden, slots, in_grad, out_grad


def solution(mesh):
    split = Mesh(mesh.devices.reshape(NY, NC, NZ, NX), ("y", "core", "z", "x"))
    dp, mp = ("y", "core"), ("z", "x")
    return jax.shard_map(
        per_device,
        mesh=split,
        in_specs=(
            P(dp + mp, None),
            P(mp, None, None, None),
            P(mp, None),
            P(mp, None, None),
            P(mp, None),
            P(None, mp),
            P(dp, mp),
        ),
        out_specs=(
            P(dp, mp),
            P(mp + dp, None, None),
            P(mp + dp, None),
            P(None, mp + dp),
        ),
        check_vma=False,
    )
```

time: 618 us -> 225 us (0.36)
  waiting for transfers between devices: 467 us -> 57.5 us
  starting transfers between devices: 0.5 us -> 91.2 us
  local copies, waits for them, and re-layouts: 73.3 us -> 12.4 us
  matrix products: 57.5 us -> 4.44 us
  Pallas kernels: 0 us -> 37.4 us
  blocking collectives: 0 us -> 18.4 us
  between operations: 14.2 us -> 1.11 us
    psum x2 -> x0, waiting for transfers between devices: 201 us -> none  [the longest x1 144 us: per_device(): lax.psum(jnp.dot(pre_grad, factor_out.T, precision=highest), 'mp')]
    all_gather x2 -> x0, waiting for transfers between devices: 160 us -> none  [the longest x1 124 us: per_device(): gathered = lax.all_gather(tokens, 'mp', axis=0, tiled=True)]
    reduce_scatter x3 -> x0, waiting for transfers between devices: 105 us -> none  [the longest x1 40.7 us: per_device(): lax.psum_scatter(block_grad, 'dp', scatter_dimension=0, tiled=True)]
    ppermute x0 -> x35, starting transfers between devices: none -> 62.1 us  [shift(): return lambda value: lax.ppermute(value, axis, pairs)]
    dot_general x7 -> x2, matrix products: 57.5 us -> 4.44 us  [the longest x1 2.23 us: per_device(): partial = jnp.einsum('sbtf,bfr->str', own_cols, factor, precision=highest)]
    pallas_call x0 -> x3, Pallas kernels: none -> 37.4 us  [the longest x1 30.5 us: per_device(): pl.pallas_call(main_kernel, grid_spec=pltpu.PrefetchScalarGridSpec(num_sc...]
    gather x3 -> x0, local copies, waits for them, and re-layouts: 31.6 us -> none  [the longest x2 28.2 us: per_device(): jnp.take(feature_blocks, block_rows.reshape(-1), axis=1).astype(jnp.float32)]
    all_to_all x0 -> x5, waiting for transfers between devices: none -> 31 us  [the longest x1 22.4 us: per_device(): in_grad = jnp.sum(lax.all_to_all(in_part, ('y', 'core'), 0, 0), axis=0)]
  transfers between devices with their start and end apart: 7 -> 40, of which waited for: 7 -> 11; matrix products, arithmetic and copies ran while one was open for 17% -> 4% of each run, Pallas kernels for 0% -> 2%
where the time goes in v1:
time: 225 us; the launch traced here: 224 us
  starting transfers between devices  91.2 us (41%)
  waiting for transfers between devices  57.5 us (26%)
  Pallas kernels  37.4 us (17%)
  blocking collectives  18.4 us (8%)
  local copies, waits for them, and re-layouts  12.4 us (6%)
  matrix products  4.44 us (2%)
    ppermute x35, starting transfers between devices, shift(): return lambda value: lax.ppermute(value, axis, pairs)  62.1 us
    pallas_call x1, Pallas kernels, per_device(): pl.pallas_call(main_kernel, grid_spec=pltpu.PrefetchScalarGridSpec(num_sc...  30.5 us
    ppermute x35, waiting for transfers between devices, shift(): return lambda value: lax.ppermute(value, axis, pairs)  26.5 us
    all_to_all x1, waiting for transfers between devices, per_device(): in_grad = jnp.sum(lax.all_to_all(in_part, ('y', 'core'), 0, 0), axis=0)  22.4 us
    all_to_all x1, blocking collectives, per_device(): lax.all_to_all(back.reshape(span, ROWS, BS), plane, 0, 0)  18.4 us
    unnamed x45, local copies, waits for them, and re-layouts  8.4 us
    all_to_all x1, starting transfers between devices, per_device(): in_grad = jnp.sum(lax.all_to_all(in_part, ('y', 'core'), 0, 0), axis=0)  7.32 us
    all_to_all x1, starting transfers between devices, per_device(): low_own = jnp.sum(lax.all_to_all(partial, plane, 0, 0), axis=0)  6.31 us
  transfers between devices with their start and end apart: 40, of which 11 were waited for; matrix products, arithmetic and copies ran while one was open for 4% of the time, Pallas kernels for 2%

profile of v1, /device:TPU:1, one launch (start us, length us, event | category | flops | bytes accessed | tf_op | source)
XLA Modules:
  0.0 224.2 jit_solution(14009864211308945609)
XLA Ops:
  2.5 6.4 %collective-permute-start.15 = (bf16[96,16,128]{2,1,0:T(8,128)(2,1)S(1)}, bf16[96,16,128]{2,1,0:T(8,128)(2,1)S(1)}, u32[]{:S(2)}, u32[]{:S(2)}) collective-permute-start(bf16[96,16,128]{2,1,0:T(8,128)(2,1)S(1)} %get-tuple-element.36.rest_13_), channel_id=1, source_target_pairs={{0,28},{4,0},{8,4},{12,8},{16,12},{20,16},{24,20},{28,24},{1,29},{... | collective-permute-start | bytes 1179656 | tf_op jit(solution)/shard_map/ppermute | solution.py:29
  8.9 2.5 %collective-permute-start.14 = (bf16[96,16,128]{2,1,0:T(8,128)(2,1)S(1)}, bf16[96,16,128]{2,1,0:T(8,128)(2,1)S(1)}, u32[]{:S(2)}, u32[]{:S(2)}) collective-permute-start(bf16[96,16,128]{2,1,0:T(8,128)(2,1)S(1)} %get-tuple-element.36.rest_13_), channel_id=1, source_target_pairs={{0,3},{1,0},{2,1},{3,2},{4,7},{5,4},{6,5},{7,6},{8,11},{9,8},{10,9... | collective-permute-start | bytes 1179656 | tf_op jit(solution)/shard_map/ppermute | solution.py:29
  11.4 1.7 collective-permute-start.5
  13.1 3.6 %collective-permute-done.15.rest_17_ = bf16[96,16,128]{2,1,0:T(8,128)(2,1)S(1)} collective-permute-done((bf16[96,16,128]{2,1,0:T(8,128)(2,1)S(1)}, bf16[96,16,128]{2,1,0:T(8,128)(2,1)S(1)}, u32[]{:S(2)}, u32[]{:S(2)}) %collective-permute-start.15) | collective-permute-done | bytes 393248 | tf_op jit(solution)/shard_map/ppermute | solution.py:29
  16.7 3.4 %collective-permute-start.19 = (bf16[96,16,128]{2,1,0:T(8,128)(2,1)S(1)}, bf16[96,16,128]{2,1,0:T(8,128)(2,1)S(1)}, u32[]{:S(2)}, u32[]{:S(2)}) collective-permute-start(bf16[96,16,128]{2,1,0:T(8,128)(2,1)S(1)} %collective-permute-done.15.rest_17_), channel_id=1, source_target_pairs={{0,28},{4,0},{8,4},{12,8},{16,12},{20,16},{24,20},{28,24},{1,29},{... | collective-permute-start | bytes 1179656 | tf_op jit(solution)/shard_map/ppermute | solution.py:29
  23.6 5.9 %collective-permute-done.5.rest_15_ = bf16[96,16,128]{2,1,0:T(8,128)(2,1)S(1)} collective-permute-done((bf16[96,16,128]{2,1,0:T(8,128)(2,1)S(1)}, bf16[96,16,128]{2,1,0:T(8,128)(2,1)S(1)}, u32[]{:S(2)}, u32[]{:S(2)}) %collective-permute-start.5) | collective-permute-done | bytes 393248 | tf_op jit(solution)/shard_map/ppermute | solution.py:29
  29.5 2.7 %collective-permute-start.18 = (bf16[96,16,128]{2,1,0:T(8,128)(2,1)S(1)}, bf16[96,16,128]{2,1,0:T(8,128)(2,1)}, u32[]{:S(2)}, u32[]{:S(2)}) collective-permute-start(bf16[96,16,128]{2,1,0:T(8,128)(2,1)S(1)} %collective-permute-done.5.rest_15_), channel_id=1, source_target_pairs={{0,28},{4,0},{8,4},{12,8},{16,12},{20,16},{24,20},{28,24},{1,29},{... | collective-permute-start | bytes 1179656 | tf_op jit(solution)/shard_map/ppermute | solution.py:29
  32.9 5.6 %all-to-all-start = ((bf16[32,3,16,128]{3,2,1,0:T(8,128)(2,1)}), bf16[32,3,16,128]{3,2,1,0:T(8,128)(2,1)S(1)}, u32[]{:S(2)}, u32[]{:S(2)}) async-start(bf16[32,3,16,128]{3,2,1,0:T(8,128)(2,1)} %bitcast.1), calls=%async_computation | async-start | bytes 786432 | tf_op jit(solution)/shard_map/all_to_all | solution.py:216
  38.8 2.3 %collective-permute-start.13 = (bf16[96,16,128]{2,1,0:T(8,128)(2,1)}, bf16[96,16,128]{2,1,0:T(8,128)(2,1)S(1)}, u32[]{:S(2)}, u32[]{:S(2)}) collective-permute-start(bf16[96,16,128]{2,1,0:T(8,128)(2,1)} %copy-done.13), channel_id=1, source_target_pairs={{0,3},{1,0},{2,1},{3,2},{4,7},{5,4},{6,5},{7,6},{8,11},{9,8},{10,9... | collective-permute-start | bytes 1179656 | tf_op jit(solution)/shard_map/ppermute | solution.py:29
  43.7 3.4 %collective-permute-start.21 = (bf16[96,16,128]{2,1,0:T(8,128)(2,1)}, bf16[96,16,128]{2,1,0:T(8,128)(2,1)S(1)}, u32[]{:S(2)}, u32[]{:S(2)}) collective-permute-start(bf16[96,16,128]{2,1,0:T(8,128)(2,1)} %copy-done.14), channel_id=1, source_target_pairs={{0,3},{1,0},{2,1},{3,2},{4,7},{5,4},{6,5},{7,6},{8,11},{9,8},{10,9... | collective-permute-start | bytes 1179656 | tf_op jit(solution)/shard_map/ppermute | solution.py:29
  48.2 2.8 %collective-permute-start.22 = (bf16[96,16,128]{2,1,0:T(8,128)(2,1)}, bf16[96,16,128]{2,1,0:T(8,128)(2,1)}, u32[]{:S(2)}, u32[]{:S(2)}) collective-permute-start(bf16[96,16,128]{2,1,0:T(8,128)(2,1)} %collective-permute-done.18.rest_19_), channel_id=1, source_target_pairs={{0,28},{4,0},{8,4},{12,8},{16,12},{20,16},{24,20},{28,24},{1,29},{... | collective-permute-start | bytes 1179656 | tf_op jit(solution)/shard_map/ppermute | solution.py:29
  51.0 9.8 %collective-permute-done.1.rest_5_ = bf16[96,16,128]{2,1,0:T(8,128)(2,1)S(1)} collective-permute-done((bf16[96,16,128]{2,1,0:T(8,128)(2,1)}, bf16[96,16,128]{2,1,0:T(8,128)(2,1)S(1)}, u32[]{:S(2)}, u32[]{:S(2)}) %collective-permute-start.1) | collective-permute-done | bytes 393248 | tf_op jit(solution)/shard_map/ppermute | solution.py:29
  63.3 2.7 %collective-permute-start.9 = (bf16[96,16,128]{2,1,0:T(8,128)(2,1)S(1)}, bf16[96,16,128]{2,1,0:T(8,128)(2,1)S(1)}, u32[]{:S(2)}, u32[]{:S(2)}) collective-permute-start(bf16[96,16,128]{2,1,0:T(8,128)(2,1)S(1)} %collective-permute-done.1.rest_5_), channel_id=1, source_target_pairs={{0,1},{1,2},{2,3},{3,0},{4,5},{5,6},{6,7},{7,4},{8,9},{9,10},{10,1... | collective-permute-start | bytes 1179656 | tf_op jit(solution)/shard_map/ppermute | solution.py:29
  66.0 2.2 convolution_bitcast_fusion
  68.3 6.3 %all-to-all-start.1 = ((f32[32,16,128]{2,1,0:T(8,128)}), f32[32,16,128]{2,1,0:T(8,128)S(1)}, u32[]{:S(2)}, u32[]{:S(2)}) async-start(f32[32,16,128]{2,1,0:T(8,128)} %convolution_bitcast_fusion), calls=%async_computation.1 | async-start | bytes 524288 | tf_op jit(solution)/shard_map/all_to_all | solution.py:220
  74.6 2.5 %collective-permute-start.25 = (bf16[96,16,128]{2,1,0:T(8,128)(2,1)}, bf16[96,16,128]{2,1,0:T(8,128)(2,1)}, u32[]{:S(2)}, u32[]{:S(2)}) collective-permute-start(bf16[96,16,128]{2,1,0:T(8,128)(2,1)} %copy-done.16), channel_id=1, source_target_pairs={{0,3},{1,0},{2,1},{3,2},{4,7},{5,4},{6,5},{7,6},{8,11},{9,8},{10,9... | collective-permute-start | bytes 1179656 | tf_op jit(solution)/shard_map/ppermute | solution.py:29
  80.8 4.7 %all-to-all-done.1 = f32[32,16,128]{2,1,0:T(8,128)S(1)} async-done(((f32[32,16,128]{2,1,0:T(8,128)}), f32[32,16,128]{2,1,0:T(8,128)S(1)}, u32[]{:S(2)}, u32[]{:S(2)}) %all-to-all-start.1) | async-done | bytes 262176 | tf_op jit(solution)/shard_map/all_to_all | solution.py:220
  86.3 5.3 %all-to-all-start.2 = ((f32[32,16,128]{2,1,0:T(8,128)}), f32[32,16,128]{2,1,0:T(8,128)S(1)}, u32[]{:S(2)}, u32[]{:S(2)}) async-start(f32[32,16,128]{2,1,0:T(8,128)} %broadcast_in_dim.15), calls=%async_computation.2 | async-start | bytes 524288 | tf_op jit(solution)/shard_map/all_to_all | solution.py:221
  91.6 2.5 %collective-permute-start.4 = (bf16[96,16,128]{2,1,0:T(8,128)(2,1)S(1)}, bf16[96,16,128]{2,1,0:T(8,128)(2,1)S(1)}, u32[]{:S(2)}, u32[]{:S(2)}) collective-permute-start(bf16[96,16,128]{2,1,0:T(8,128)(2,1)S(1)} %collective-permute-done.2.rest_1_), channel_id=1, source_target_pairs={{0,3},{1,0},{2,1},{3,2},{4,7},{5,4},{6,5},{7,6},{8,11},{9,8},{10,9... | collective-permute-start | bytes 1179656 | tf_op jit(solution)/shard_map/ppermute | solution.py:29
  94.1 2.7 %collective-permute-start.29 = (bf16[96,16,128]{2,1,0:T(8,128)(2,1)}, bf16[96,16,128]{2,1,0:T(8,128)(2,1)}, u32[]{:S(2)}, u32[]{:S(2)}) collective-permute-start(bf16[96,16,128]{2,1,0:T(8,128)(2,1)} %collective-permute-done.27.rest_29_), channel_id=1, source_target_pairs={{0,3},{1,0},{2,1},{3,2},{4,7},{5,4},{6,5},{7,6},{8,11},{9,8},{10,9... | collective-permute-start | bytes 1179656 | tf_op jit(solution)/shard_map/ppermute | solution.py:29
  100.4 2.5 %collective-permute-done.3.rest_0_ = bf16[96,16,128]{2,1,0:T(8,128)(2,1)S(1)} collective-permute-done((bf16[96,16,128]{2,1,0:T(8,128)(2,1)S(1)}, bf16[96,16,128]{2,1,0:T(8,128)(2,1)S(1)}, u32[]{:S(2)}, u32[]{:S(2)}) %collective-permute-start.3) | collective-permute-done | bytes 393248 | tf_op jit(solution)/shard_map/ppermute | solution.py:29
  103.7 3.9 %all-to-all-done.2 = f32[32,16,128]{2,1,0:T(8,128)S(1)} async-done(((f32[32,16,128]{2,1,0:T(8,128)}), f32[32,16,128]{2,1,0:T(8,128)S(1)}, u32[]{:S(2)}, u32[]{:S(2)}) %all-to-all-start.2) | async-done | bytes 262176 | tf_op jit(solution)/shard_map/all_to_all | solution.py:221
  110.8 30.5 %columns.1 = (bf16[512,1536]{1,0:T(8,128)(2,1)}, s16[4,2528,128]{2,1,0:T(8,128)(2,1)}, s16[4,2528,128]{2,1,0:T(8,128)(2,1)}, f32[512,128]{1,0:T(8,128)S(1)}) custom-call(s32[96]{0:T(128)S(1)} %reshape.179.rows_ref, s32[4,96]{1,0:T(4,128)S(1)} %pad_add_fusion.where_ref, s32[32]{0:T(128)S(1)} %stack.148.place_ref, f32[512,128]{1,0:T(8,128)S(1)} %bitcast.86, ...), custom_call_target="tpu_custom_call" | custom-call | tf_op jit(solution)/shard_map/columns/pallas_call | solution.py:256
  141.3 11.4 %collective-permute-start.31 = (s16[4,2528,128]{2,1,0:T(8,128)(2,1)}, s16[4,2528,128]{2,1,0:T(8,128)(2,1)S(1)}, u32[]{:S(2)}, u32[]{:S(2)}) collective-permute-start(s16[4,2528,128]{2,1,0:T(8,128)(2,1)} %get-tuple-element.12), channel_id=1, source_target_pairs={{0,32},{32,0},{1,33},{33,1},{2,34},{34,2},{3,35},{35,3},{4,36},{36... | collective-permute-start | bytes 7766024 | tf_op jit(solution)/shard_map/ppermute | solution.py:29
  152.7 18.4 %all_to_all.30 = f32[32,16,128]{2,1,0:T(8,128)S(1)} all-to-all(f32[32,16,128]{2,1,0:T(8,128)S(1)} %bitcast.87), channel_id=1, replica_groups=mesh['y'=4,'core'=2,'z'=8,'x'=4] {'z','x'}, dimensions={0} | all-to-all | bytes 524288 | tf_op jit(solution)/shard_map/all_to_all | solution.py:313
  171.9 4.6 %all-to-all-start.4 = ((f32[32,16,128]{2,1,0:T(8,128)}), f32[32,16,128]{2,1,0:T(8,128)}, u32[]{:S(2)}, u32[]{:S(2)}) async-start(f32[32,16,128]{2,1,0:T(8,128)} %broadcast_in_dim.18), calls=%async_computation.4 | async-start | bytes 524288 | tf_op jit(solution)/shard_map/all_to_all | solution.py:314
  178.1 4.6 %pairs.1 = s16[4,2528,128]{2,1,0:T(8,128)(2,1)S(1)} custom-call(s16[4,2528,128]{2,1,0:T(8,128)(2,1)} %get-tuple-element.11.keep_ref, s16[4,2528,128]{2,1,0:T(8,128)(2,1)} %copy-done.7), custom_call_target="tpu_custom_call" | custom-call | tf_op jit(solution)/shard_map/pairs/pallas_call | solution.py:297
  184.0 2.7 %collective-permute-start.34 = (s16[2528,128]{1,0:T(8,128)(2,1)}, s16[2528,128]{1,0:T(8,128)(2,1)S(1)}, u32[]{:S(2)}, u32[]{:S(2)}) collective-permute-start(s16[2528,128]{1,0:T(8,128)(2,1)} %get-tuple-element.32), channel_id=1, source_target_pairs={{0,192},{64,0},{128,64},{192,128},{1,193},{65,1},{129,65},{193,129... | collective-permute-start | bytes 1941512 | tf_op jit(solution)/shard_map/ppermute | solution.py:29
  187.7 2.2 fusion
  189.9 7.3 %all-to-all-start.5 = ((f32[8,48,128]{2,1,0:T(8,128)}), f32[8,48,128]{2,1,0:T(8,128)S(1)}, u32[]{:S(2)}, u32[]{:S(2)}) async-start(f32[8,48,128]{2,1,0:T(8,128)} %bitcast.88), calls=%async_computation.5 | async-start | bytes 393216 | tf_op jit(solution)/shard_map/all_to_all | solution.py:319
  198.0 22.4 %all-to-all-done.5 = f32[8,48,128]{2,1,0:T(8,128)S(1)} async-done(((f32[8,48,128]{2,1,0:T(8,128)}), f32[8,48,128]{2,1,0:T(8,128)S(1)}, u32[]{:S(2)}, u32[]{:S(2)}) %all-to-all-start.5) | async-done | bytes 196640 | tf_op jit(solution)/shard_map/all_to_all | solution.py:319
  221.1 2.4 %slots.1 = (f32[18,128,128]{2,1,0:T(8,128)}, f32[128,192]{1,0:T(8,128)S(1)}) custom-call(s32[1]{0:T(128)} %bitcast.43.count_ref, s16[2528,128]{1,0:T(8,128)(2,1)S(1)} %get-tuple-element.35.refs_0_, s16[2528,128]{1,0:T(8,128)(2,1)S(1)} %collective-permute-done.32.refs_1_, s16[2528,128]{1,0:T(8,128)(2,1)S(1)} %collective-permute-done.33.refs_2_, ...), custom_call_target="tpu_custom_call" | custom-call | tf_op jit(solution)/shard_map/slots/pallas_call | solution.py:322
  (118 shorter events, 31.2 us)
Async XLA Ops:
  2.5 14.2 %collective-permute-start.15 = (bf16[96,16,128]{2,1,0:T(8,128)(2,1)S(1)}, bf16[96,16,128]{2,1,0:T(8,128)(2,1)S(1)}, u32[]{:S(2)}, u32[]{:S(2)}) collective-permute-start(bf16[96,16,128]{2,1,0:T(8,128)(2,1)S(1)} %get-tuple-element.36.rest_13_), channel_id=1, source_target_pairs={{0,28},{4,0},{8,4},{12,8},{16,12},{20,16},{24,20},{28,24},{1,29},{... | collective-permute-start | bytes 1179656 | tf_op jit(solution)/shard_map/ppermute | solution.py:29
  11.4 18.1 %collective-permute-start.5 = (bf16[96,16,128]{2,1,0:T(8,128)(2,1)S(1)}, bf16[96,16,128]{2,1,0:T(8,128)(2,1)S(1)}, u32[]{:S(2)}, u32[]{:S(2)}) collective-permute-start(bf16[96,16,128]{2,1,0:T(8,128)(2,1)S(1)} %get-tuple-element.36.rest_13_), channel_id=1, source_target_pairs={{0,2},{1,3},{2,0},{3,1},{4,6},{5,7},{6,4},{7,5},{8,10},{9,11},{10,... | collective-permute-start | bytes 1179656 | tf_op jit(solution)/shard_map/ppermute | solution.py:29
  13.1 16.4 %collective-permute-start = (bf16[96,16,128]{2,1,0:T(8,128)(2,1)S(1)}, bf16[96,16,128]{2,1,0:T(8,128)(2,1)S(1)}, u32[]{:S(2)}, u32[]{:S(2)}) collective-permute-start(bf16[96,16,128]{2,1,0:T(8,128)(2,1)S(1)} %get-tuple-element.36.rest_13_), channel_id=1, source_target_pairs={{0,4},{4,8},{8,12},{12,16},{16,20},{20,24},{24,28},{28,0},{1,5},{5... | collective-permute-start | bytes 1179656 | tf_op jit(solution)/shard_map/ppermute | solution.py:29
  16.7 15.5 %collective-permute-start.19 = (bf16[96,16,128]{2,1,0:T(8,128)(2,1)S(1)}, bf16[96,16,128]{2,1,0:T(8,128)(2,1)S(1)}, u32[]{:S(2)}, u32[]{:S(2)}) collective-permute-start(bf16[96,16,128]{2,1,0:T(8,128)(2,1)S(1)} %collective-permute-done.15.rest_17_), channel_id=1, source_target_pairs={{0,28},{4,0},{8,4},{12,8},{16,12},{20,16},{24,20},{28,24},{1,29},{... | collective-permute-start | bytes 1179656 | tf_op jit(solution)/shard_map/ppermute | solution.py:29
  20.1 18.7 %collective-permute-start.16 = (bf16[96,16,128]{2,1,0:T(8,128)(2,1)S(1)}, bf16[96,16,128]{2,1,0:T(8,128)(2,1)}, u32[]{:S(2)}, u32[]{:S(2)}) collective-permute-start(bf16[96,16,128]{2,1,0:T(8,128)(2,1)S(1)} %collective-permute-done.15.rest_17_), channel_id=1, source_target_pairs={{0,1},{1,2},{2,3},{3,0},{4,5},{5,6},{6,7},{7,4},{8,9},{9,10},{10,1... | collective-permute-start | bytes 1179656 | tf_op jit(solution)/shard_map/ppermute | solution.py:29
  22.9 18.2 %collective-permute-start.17 = (bf16[96,16,128]{2,1,0:T(8,128)(2,1)S(1)}, bf16[96,16,128]{2,1,0:T(8,128)(2,1)}, u32[]{:S(2)}, u32[]{:S(2)}) collective-permute-start(bf16[96,16,128]{2,1,0:T(8,128)(2,1)S(1)} %collective-permute-done.14.rest_14_), channel_id=1, source_target_pairs={{0,28},{4,0},{8,4},{12,8},{16,12},{20,16},{24,20},{28,24},{1,29},{... | collective-permute-start | bytes 1179656 | tf_op jit(solution)/shard_map/ppermute | solution.py:29
  29.5 14.2 %collective-permute-start.18 = (bf16[96,16,128]{2,1,0:T(8,128)(2,1)S(1)}, bf16[96,16,128]{2,1,0:T(8,128)(2,1)}, u32[]{:S(2)}, u32[]{:S(2)}) collective-permute-start(bf16[96,16,128]{2,1,0:T(8,128)(2,1)S(1)} %collective-permute-done.5.rest_15_), channel_id=1, source_target_pairs={{0,28},{4,0},{8,4},{12,8},{16,12},{20,16},{24,20},{28,24},{1,29},{... | collective-permute-start | bytes 1179656 | tf_op jit(solution)/shard_map/ppermute | solution.py:29
  32.9 14.2 %collective-permute-start.6 = (bf16[96,16,128]{2,1,0:T(8,128)(2,1)S(1)}, bf16[96,16,128]{2,1,0:T(8,128)(2,1)}, u32[]{:S(2)}, u32[]{:S(2)}) collective-permute-start(bf16[96,16,128]{2,1,0:T(8,128)(2,1)S(1)} %collective-permute-done.5.rest_15_), channel_id=1, source_target_pairs={{0,4},{4,8},{8,12},{12,16},{16,20},{20,24},{24,28},{28,0},{1,5},{5... | collective-permute-start | bytes 1179656 | tf_op jit(solution)/shard_map/ppermute | solution.py:29
  32.9 33.1 %all-to-all-start = ((bf16[32,3,16,128]{3,2,1,0:T(8,128)(2,1)}), bf16[32,3,16,128]{3,2,1,0:T(8,128)(2,1)S(1)}, u32[]{:S(2)}, u32[]{:S(2)}) async-start(bf16[32,3,16,128]{3,2,1,0:T(8,128)(2,1)} %bitcast.1), calls=%async_computation | async-start | bytes 786432 | tf_op jit(solution)/shard_map/all_to_all | solution.py:216
  41.1 19.8 %collective-permute-start.1 = (bf16[96,16,128]{2,1,0:T(8,128)(2,1)}, bf16[96,16,128]{2,1,0:T(8,128)(2,1)S(1)}, u32[]{:S(2)}, u32[]{:S(2)}) collective-permute-start(bf16[96,16,128]{2,1,0:T(8,128)(2,1)} %copy-done.13), channel_id=1, source_target_pairs={{0,4},{4,8},{8,12},{12,16},{16,20},{20,24},{24,28},{28,0},{1,5},{5... | collective-permute-start | bytes 1179656 | tf_op jit(solution)/shard_map/ppermute | solution.py:29
  42.2 18.6 %collective-permute-start.23 = (bf16[96,16,128]{2,1,0:T(8,128)(2,1)}, bf16[96,16,128]{2,1,0:T(8,128)(2,1)S(1)}, u32[]{:S(2)}, u32[]{:S(2)}) collective-permute-start(bf16[96,16,128]{2,1,0:T(8,128)(2,1)} %copy-done.14), channel_id=1, source_target_pairs={{0,28},{4,0},{8,4},{12,8},{16,12},{20,16},{24,20},{28,24},{1,29},{... | collective-permute-start | bytes 1179656 | tf_op jit(solution)/shard_map/ppermute | solution.py:29
  43.7 17.2 %collective-permute-start.21 = (bf16[96,16,128]{2,1,0:T(8,128)(2,1)}, bf16[96,16,128]{2,1,0:T(8,128)(2,1)S(1)}, u32[]{:S(2)}, u32[]{:S(2)}) collective-permute-start(bf16[96,16,128]{2,1,0:T(8,128)(2,1)} %copy-done.14), channel_id=1, source_target_pairs={{0,3},{1,0},{2,1},{3,2},{4,7},{5,4},{6,5},{7,6},{8,11},{9,8},{10,9... | collective-permute-start | bytes 1179656 | tf_op jit(solution)/shard_map/ppermute | solution.py:29
  47.1 15.4 %collective-permute-start.20 = (bf16[96,16,128]{2,1,0:T(8,128)(2,1)}, bf16[96,16,128]{2,1,0:T(8,128)(2,1)S(1)}, u32[]{:S(2)}, u32[]{:S(2)}) collective-permute-start(bf16[96,16,128]{2,1,0:T(8,128)(2,1)} %copy-done.14), channel_id=1, source_target_pairs={{0,1},{1,2},{2,3},{3,0},{4,5},{5,6},{6,7},{7,4},{8,9},{9,10},{10,1... | collective-permute-start | bytes 1179656 | tf_op jit(solution)/shard_map/ppermute | solution.py:29
  48.2 26.3 %collective-permute-start.22 = (bf16[96,16,128]{2,1,0:T(8,128)(2,1)}, bf16[96,16,128]{2,1,0:T(8,128)(2,1)}, u32[]{:S(2)}, u32[]{:S(2)}) collective-permute-start(bf16[96,16,128]{2,1,0:T(8,128)(2,1)} %collective-permute-done.18.rest_19_), channel_id=1, source_target_pairs={{0,28},{4,0},{8,4},{12,8},{16,12},{20,16},{24,20},{28,24},{1,29},{... | collective-permute-start | bytes 1179656 | tf_op jit(solution)/shard_map/ppermute | solution.py:29
  60.8 16.3 %collective-permute-start.7 = (bf16[96,16,128]{2,1,0:T(8,128)(2,1)}, bf16[96,16,128]{2,1,0:T(8,128)(2,1)S(1)}, u32[]{:S(2)}, u32[]{:S(2)}) collective-permute-start(bf16[96,16,128]{2,1,0:T(8,128)(2,1)} %collective-permute-done.6.rest_11_), channel_id=1, source_target_pairs={{0,4},{4,8},{8,12},{12,16},{16,20},{20,24},{24,28},{28,0},{1,5},{5... | collective-permute-start | bytes 1179656 | tf_op jit(solution)/shard_map/ppermute | solution.py:29
  60.8 16.3 %collective-permute-start.2 = (bf16[96,16,128]{2,1,0:T(8,128)(2,1)S(1)}, bf16[96,16,128]{2,1,0:T(8,128)(2,1)S(1)}, u32[]{:S(2)}, u32[]{:S(2)}) collective-permute-start(bf16[96,16,128]{2,1,0:T(8,128)(2,1)S(1)} %collective-permute-done.1.rest_5_), channel_id=1, source_target_pairs={{0,4},{4,8},{8,12},{12,16},{16,20},{20,24},{24,28},{28,0},{1,5},{5... | collective-permute-start | bytes 1179656 | tf_op jit(solution)/shard_map/ppermute | solution.py:29
  61.0 17.4 %collective-permute-start.10 = (bf16[96,16,128]{2,1,0:T(8,128)(2,1)S(1)}, bf16[96,16,128]{2,1,0:T(8,128)(2,1)S(1)}, u32[]{:S(2)}, u32[]{:S(2)}) collective-permute-start(bf16[96,16,128]{2,1,0:T(8,128)(2,1)S(1)} %collective-permute-done.1.rest_5_), channel_id=1, source_target_pairs={{0,3},{1,0},{2,1},{3,2},{4,7},{5,4},{6,5},{7,6},{8,11},{9,8},{10,9... | collective-permute-start | bytes 1179656 | tf_op jit(solution)/shard_map/ppermute | solution.py:29
  63.3 16.6 %collective-permute-start.9 = (bf16[96,16,128]{2,1,0:T(8,128)(2,1)S(1)}, bf16[96,16,128]{2,1,0:T(8,128)(2,1)S(1)}, u32[]{:S(2)}, u32[]{:S(2)}) collective-permute-start(bf16[96,16,128]{2,1,0:T(8,128)(2,1)S(1)} %collective-permute-done.1.rest_5_), channel_id=1, source_target_pairs={{0,1},{1,2},{2,3},{3,0},{4,5},{5,6},{6,7},{7,4},{8,9},{9,10},{10,1... | collective-permute-start | bytes 1179656 | tf_op jit(solution)/shard_map/ppermute | solution.py:29
  68.3 17.2 %all-to-all-start.1 = ((f32[32,16,128]{2,1,0:T(8,128)}), f32[32,16,128]{2,1,0:T(8,128)S(1)}, u32[]{:S(2)}, u32[]{:S(2)}) async-start(f32[32,16,128]{2,1,0:T(8,128)} %convolution_bitcast_fusion), calls=%async_computation.1 | async-start | bytes 524288 | tf_op jit(solution)/shard_map/all_to_all | solution.py:220
  74.6 17.0 %collective-permute-start.25 = (bf16[96,16,128]{2,1,0:T(8,128)(2,1)}, bf16[96,16,128]{2,1,0:T(8,128)(2,1)}, u32[]{:S(2)}, u32[]{:S(2)}) collective-permute-start(bf16[96,16,128]{2,1,0:T(8,128)(2,1)} %copy-done.16), channel_id=1, source_target_pairs={{0,3},{1,0},{2,1},{3,2},{4,7},{5,4},{6,5},{7,6},{8,11},{9,8},{10,9... | collective-permute-start | bytes 1179656 | tf_op jit(solution)/shard_map/ppermute | solution.py:29
  77.1 17.0 %collective-permute-start.24 = (bf16[96,16,128]{2,1,0:T(8,128)(2,1)}, bf16[96,16,128]{2,1,0:T(8,128)(2,1)}, u32[]{:S(2)}, u32[]{:S(2)}) collective-permute-start(bf16[96,16,128]{2,1,0:T(8,128)(2,1)} %copy-done.16), channel_id=1, source_target_pairs={{0,1},{1,2},{2,3},{3,0},{4,5},{5,6},{6,7},{7,4},{8,9},{9,10},{10,1... | collective-permute-start | bytes 1179656 | tf_op jit(solution)/shard_map/ppermute | solution.py:29
  77.1 17.0 %collective-permute-start.27 = (bf16[96,16,128]{2,1,0:T(8,128)(2,1)S(1)}, bf16[96,16,128]{2,1,0:T(8,128)(2,1)}, u32[]{:S(2)}, u32[]{:S(2)}) collective-permute-start(bf16[96,16,128]{2,1,0:T(8,128)(2,1)S(1)} %collective-permute-done.2.rest_1_), channel_id=1, source_target_pairs={{0,4},{4,8},{8,12},{12,16},{16,20},{20,24},{24,28},{28,0},{1,5},{5... | collective-permute-start | bytes 1179656 | tf_op jit(solution)/shard_map/ppermute | solution.py:29
  78.4 18.4 %collective-permute-start.26 = (bf16[96,16,128]{2,1,0:T(8,128)(2,1)}, bf16[96,16,128]{2,1,0:T(8,128)(2,1)}, u32[]{:S(2)}, u32[]{:S(2)}) collective-permute-start(bf16[96,16,128]{2,1,0:T(8,128)(2,1)} %collective-permute-done.22.rest_23_), channel_id=1, source_target_pairs={{0,28},{4,0},{8,4},{12,8},{16,12},{20,16},{24,20},{28,24},{1,29},{... | collective-permute-start | bytes 1179656 | tf_op jit(solution)/shard_map/ppermute | solution.py:29
  79.9 18.6 %collective-permute-start.8 = (bf16[96,16,128]{2,1,0:T(8,128)(2,1)S(1)}, bf16[96,16,128]{2,1,0:T(8,128)(2,1)S(1)}, u32[]{:S(2)}, u32[]{:S(2)}) collective-permute-start(bf16[96,16,128]{2,1,0:T(8,128)(2,1)S(1)} %collective-permute-done.7.rest_7_), channel_id=1, source_target_pairs={{0,4},{4,8},{8,12},{12,16},{16,20},{20,24},{24,28},{28,0},{1,5},{5... | collective-permute-start | bytes 1179656 | tf_op jit(solution)/shard_map/ppermute | solution.py:29
  86.3 21.4 %all-to-all-start.2 = ((f32[32,16,128]{2,1,0:T(8,128)}), f32[32,16,128]{2,1,0:T(8,128)S(1)}, u32[]{:S(2)}, u32[]{:S(2)}) async-start(f32[32,16,128]{2,1,0:T(8,128)} %broadcast_in_dim.15), calls=%async_computation.2 | async-start | bytes 524288 | tf_op jit(solution)/shard_map/all_to_all | solution.py:221
  94.1 14.7 %collective-permute-start.29 = (bf16[96,16,128]{2,1,0:T(8,128)(2,1)}, bf16[96,16,128]{2,1,0:T(8,128)(2,1)}, u32[]{:S(2)}, u32[]{:S(2)}) collective-permute-start(bf16[96,16,128]{2,1,0:T(8,128)(2,1)} %collective-permute-done.27.rest_29_), channel_id=1, source_target_pairs={{0,3},{1,0},{2,1},{3,2},{4,7},{5,4},{6,5},{7,6},{8,11},{9,8},{10,9... | collective-permute-start | bytes 1179656 | tf_op jit(solution)/shard_map/ppermute | solution.py:29
  141.3 35.2 %collective-permute-start.31 = (s16[4,2528,128]{2,1,0:T(8,128)(2,1)}, s16[4,2528,128]{2,1,0:T(8,128)(2,1)S(1)}, u32[]{:S(2)}, u32[]{:S(2)}) collective-permute-start(s16[4,2528,128]{2,1,0:T(8,128)(2,1)} %get-tuple-element.12), channel_id=1, source_target_pairs={{0,32},{32,0},{1,33},{33,1},{2,34},{34,2},{3,35},{35,3},{4,36},{36... | collective-permute-start | bytes 7766024 | tf_op jit(solution)/shard_map/ppermute | solution.py:29
  171.9 15.8 %all-to-all-start.4 = ((f32[32,16,128]{2,1,0:T(8,128)}), f32[32,16,128]{2,1,0:T(8,128)}, u32[]{:S(2)}, u32[]{:S(2)}) async-start(f32[32,16,128]{2,1,0:T(8,128)} %broadcast_in_dim.18), calls=%async_computation.4 | async-start | bytes 524288 | tf_op jit(solution)/shard_map/all_to_all | solution.py:314
  184.0 37.1 %collective-permute-start.34 = (s16[2528,128]{1,0:T(8,128)(2,1)}, s16[2528,128]{1,0:T(8,128)(2,1)S(1)}, u32[]{:S(2)}, u32[]{:S(2)}) collective-permute-start(s16[2528,128]{1,0:T(8,128)(2,1)} %get-tuple-element.32), channel_id=1, source_target_pairs={{0,192},{64,0},{128,64},{192,128},{1,193},{65,1},{129,65},{193,129... | collective-permute-start | bytes 1941512 | tf_op jit(solution)/shard_map/ppermute | solution.py:29
  186.7 34.4 %collective-permute-start.33 = (s16[2528,128]{1,0:T(8,128)(2,1)}, s16[2528,128]{1,0:T(8,128)(2,1)S(1)}, u32[]{:S(2)}, u32[]{:S(2)}) collective-permute-start(s16[2528,128]{1,0:T(8,128)(2,1)} %get-tuple-element.33), channel_id=1, source_target_pairs={{0,128},{64,192},{128,0},{192,64},{1,129},{65,193},{129,1},{193,65... | collective-permute-start | bytes 1941512 | tf_op jit(solution)/shard_map/ppermute | solution.py:29
  187.0 34.0 %collective-permute-start.32 = (s16[2528,128]{1,0:T(8,128)(2,1)}, s16[2528,128]{1,0:T(8,128)(2,1)S(1)}, u32[]{:S(2)}, u32[]{:S(2)}) collective-permute-start(s16[2528,128]{1,0:T(8,128)(2,1)} %get-tuple-element.34), channel_id=1, source_target_pairs={{0,64},{64,128},{128,192},{192,0},{1,65},{65,129},{129,193},{193,1... | collective-permute-start | bytes 1941512 | tf_op jit(solution)/shard_map/ppermute | solution.py:29
  189.9 30.5 %all-to-all-start.5 = ((f32[8,48,128]{2,1,0:T(8,128)}), f32[8,48,128]{2,1,0:T(8,128)S(1)}, u32[]{:S(2)}, u32[]{:S(2)}) async-start(f32[8,48,128]{2,1,0:T(8,128)} %bitcast.88), calls=%async_computation.5 | async-start | bytes 393216 | tf_op jit(solution)/shard_map/all_to_all | solution.py:319
  (29 other events, 458.1 us)
